TPU v7x, 128 devices: a whole 4x4x4 slice. The times are simulated.
128 devices in a mesh: comp: 4 (over x_hi, core), tile: 32 (over x_lo, z, y).
Axes of the slice: x: 4 (x_hi: 2, x_lo: 2; x = x_hi * 2 + x_lo), y: 4, z: 4, core: 2. Of those that a mesh axis runs over, the one named last changes fastest.
Arguments:
- state: float32 [60, 128, 24576], P(None, 'comp', 'tile'), may hold values from -6 to 6
- kappa: float32 [128, 24576], P('comp', 'tile'), may hold values from 0.03 to 0.24
- land_mask: int32 [128, 24576], P('comp', 'tile'), may hold values 0 or 1
- remap_weight: bfloat16 [16384, 128, 128], P(('comp', 'tile')), may hold values from -0.5 to 0.5
- remap_src: int32 [16384], P(('comp', 'tile')), may hold values from 0 to 191
- remap_tile: int32 [16384, 1], P(('comp', 'tile')), may hold values from 0 to 31; in each aligned block of 128 rows (0 to 127, 128 to 255, ...) at most 6 rows name the same one
- remap_block: int32 [16384], P(('comp', 'tile')), may hold values from 0 to 575
- remap_count: int32 [128], P(('comp', 'tile')), may hold values from 64 to 128, as said below
Outputs:
- state_next: float32 [60, 128, 24576], P(None, 'comp', 'tile')
Inputs may be any that keep to these rules, and one draw needn't show every extreme that they name: `remap_tile`: each device's 128 entries name no tile more than 6 times. `remap_count`: some device has all 128 blocks live.
All inputs are finite; a program needn't handle non-finite values. No bound on the sum of `land_mask` on one device may be relied on, other than what follows from the above.
Results may differ from a plain program's by a relative error of at most 0.0003.
Values sent between devices are 32-bit elements; how exact they have to be, the bound alone decides.
A program may use at most 128 MiB of HBM per device.

v0:
```python
import jax
import jax.numpy as jnp
from jax import lax
from jax.experimental import pallas as pl
from jax.experimental.pallas import tpu as pltpu
from jax.sharding import PartitionSpec as P

LEVELS = 60
COUPLED = 3
DEEP = LEVELS - COUPLED
BLK = 128
BY = 32
BX = 768
HALO = 4
TALL = BY + 2 * HALO
TOP = HALO + BY
SLOTS = 128
CAP = 6
PAIR = 7
TILES = 32
OCEAN = 3
BLOCKS = 192
COLS = BX // BLK
HALF = COLS // 2
WIDE = BX + BLK
KAPPA, SEA = 3, 4
LANES = 64
FIRST = 8
LAST = FIRST + HALF * BLK
LONG = LAST + 8
STRIDE = 49
WEIGHT_CHUNKS = 4
GROUP = min(16, TILES)
MESH = pl.DeviceIdType.MESH
F32 = jnp.float32
BF16 = jnp.bfloat16


def iota(shape, axis):
    return lax.broadcasted_iota(jnp.int32, shape, axis)


def split(x):
    high = x.astype(BF16)
    return high, (x - high.astype(F32)).astype(BF16)


def dot(a, b):
    return jnp.dot(a, b, preferred_element_type=F32)


def to_column(row):
    eye = iota((BLK, BLK), 0) == iota((BLK, BLK), 1)
    return jnp.sum(jnp.where(eye, row, 0.0), axis=1, keepdims=True)


def block_place(block):
    row = jnp.floor((block + 0.5) * (1.0 / COLS))
    return (block - COLS * row) * BY + row


def own(ref, *lead):
    return ref[lead + (pl.ds(HALO, BY), slice(None))]


def level_rows(slab, group, y):
    return pl.ds((slab * LANES + group * 8) * TALL + y, 8, stride=TALL)


def as_rows(ref):
    return ref.reshape(COLS * LANES * TALL, BLK)


def wide(ref, *lead):
    return jnp.concatenate([ref[lead + (j,)] for j in range(COLS + 1)], axis=1)


def neighbours(v):
    return (pltpu.roll(v, 1, 1) + pltpu.roll(v, WIDE - 1, 1)) + (
        pltpu.roll(v, 1, 0) + pltpu.roll(v, TALL - 1, 0)
    )


def step_rows(old, new, around, centre, y0, count):
    def load(ref, y, i):
        return ref[y0 + y, pl.ds(HALO + i, 8, stride=STRIDE), :]

    def one(i, carry):
        here, before = carry
        ahead = [load(old, y, i + 1) for y in range(-1, count + 1)]
        diagonal = [here[y] + ahead[y + 1] for y in range(count + 1)]
        for y in range(count):
            near = before[y] + diagonal[y]
            new[y0 + y, pl.ds(HALO + i, 8, stride=STRIDE), :] = (
                load(centre, y, i) * here[y + 1] + load(around, y, i) * near
            )
        return ahead, diagonal[1:]

    behind = [load(old, y, -1) for y in range(count)]
    here = [load(old, y, 0) for y in range(-1, count + 1)]
    before = [behind[y] + here[y + 2] for y in range(count)]
    lax.fori_loop(0, STRIDE, one, (here, before), unroll=7)


def step_blocks(old, new, around, centre, start, count, last, blocks):
    def one(b, carry):
        step_rows(old, new, around, centre, jnp.minimum(start + count * b, last), count)
        return carry

    lax.fori_loop(*blocks, one, 0)


def exchange_kernel(
    state, kappa, mask, weight, src, tile_of, block_of, count,
    natural, planes, sides, coef, field, around, centre,
    other, ends, weights, mask_in, small, send, received, contrib,
    load_sem, weight_sem, state_sem, remap_send, remap_recv, row_sem, side_sem,
):
    comp = lax.axis_index("comp")
    tile = lax.axis_index("tile")
    right = lax.rem(tile + 1, TILES)
    left = lax.rem(tile + TILES - 1, TILES)
    is_ocean = comp == OCEAN
    has_up = comp < OCEAN - 1
    has_down = (comp > 0) & (comp < OCEAN)

    loads = [
        pltpu.make_async_copy(part, small.at[n], load_sem.at[n])
        for n, part in enumerate((src, tile_of, block_of))
    ]
    surface_loads, kappa_loads, state_loads = [], [], []
    for j in range(COLS):
        cut = pl.ds(j * BLK, BLK)
        surface_loads.append(
            pltpu.make_async_copy(
                state.at[pl.ds(0, COUPLED), :, cut],
                planes.at[pl.ds(0, COUPLED), j, pl.ds(HALO, BY), :],
                load_sem.at[4 + j],
            )
        )
        kappa_loads.append(
            pltpu.make_async_copy(
                kappa.at[:, cut], planes.at[KAPPA, j, pl.ds(HALO, BY), :], load_sem.at[10 + j]
            )
        )
        state_loads.append(
            pltpu.make_async_copy(
                state.at[pl.ds(COUPLED, DEEP), :, cut],
                natural.at[j, pl.ds(0, DEEP), pl.ds(0, BY), :],
                state_sem.at[j],
            )
        )
    mask_load = pltpu.make_async_copy(mask, mask_in, load_sem.at[16])
    per = SLOTS // WEIGHT_CHUNKS
    weight_loads = [
        pltpu.make_async_copy(weight.at[pl.ds(n * per, per)], weights.at[pl.ds(n * per, per)], weight_sem.at[n])
        for n in range(WEIGHT_CHUNKS)
    ]
    for copy in loads + surface_loads + weight_loads + kappa_loads + [mask_load] + state_loads:
        copy.start()

    barrier = pltpu.get_barrier_semaphore()

    def greet(c, t):
        pl.semaphore_signal(barrier, inc=1, device_id=(c, t), device_id_type=MESH)

    greet(comp, left)
    greet(comp, right)

    @pl.when(has_up)
    def _():
        for t in (tile, left, right):
            greet(comp + 1, t)

    @pl.when(has_down)
    def _():
        for t in (tile, left, right):
            greet(comp - 1, t)

    @pl.when(is_ocean)
    def _():
        def body(i, carry):
            greet(i // TILES, lax.rem(i + tile, TILES))
            return carry

        lax.fori_loop(0, OCEAN * TILES, body, 0)

    @pl.when(jnp.logical_not(is_ocean))
    def _():
        def body(i, carry):
            greet(OCEAN, lax.rem(i + tile, TILES))
            return carry

        lax.fori_loop(0, TILES, body, 0)

    received[:, PAIR:, :] = jnp.zeros((received.shape[0], 8 - PAIR, received.shape[2]), F32)

    for copy in loads + surface_loads:
        copy.wait()
    surface = jnp.concatenate(
        [
            jnp.concatenate(
                [own(planes, f, j) for j in range(COLS)] + [jnp.zeros((64, BLK), F32)], axis=0
            )
            for f in range(COUPLED)
        ],
        axis=1,
    ).astype(BF16)
    src_place = to_column(block_place(small[0].astype(F32)))
    gather = (iota((BLK, 256), 1).astype(F32) == src_place).astype(BF16)
    picked_all = dot(gather, surface)
    sub = iota((32, BLK), 0) % 8
    for n in range(WEIGHT_CHUNKS):
        weight_loads[n].wait()
        for g in range(per // 8):
            base = n * per + g * 8
            picked = picked_all[base : base + 8]
            lhs = jnp.concatenate(
                [picked[:, f * BLK : (f + 1) * BLK] for f in range(COUPLED)] + [jnp.zeros((8, BLK), F32)], axis=0
            )
            spread = jnp.concatenate([jnp.where(sub == k, lhs, 0.0) for k in range(8)], axis=1).astype(BF16)
            product = dot(spread, weights[pl.ds(base, 8)].reshape(8 * BLK, BLK))
            for f in range(COUPLED):
                contrib[pl.ds(base, 8), f * BLK : (f + 1) * BLK] = product[8 * f : 8 * f + 8]

    ocean_f = jnp.where(is_ocean, 1.0, 0.0)
    active = iota((1, BLK), 1) < count[0]
    tile_row = small[1].astype(F32)
    tile_col = to_column(tile_row)
    same = tile_col == tile_row
    sub_i, lane_i = iota((BLK, BLK), 0), iota((BLK, BLK), 1)
    order_row = jnp.sum(jnp.where(same & (sub_i < lane_i), 1.0, 0.0), axis=0, keepdims=True)
    order_col = jnp.sum(jnp.where(same & (lane_i < sub_i), 1.0, 0.0), axis=1, keepdims=True)
    slot_iota = iota((TILES * 8, BLK), 0).astype(F32)
    place = (slot_iota == jnp.where(active, tile_row * 8.0 + order_row, -1.0)).astype(BF16)
    block = small[2].astype(F32)
    strip = jnp.floor((block + 0.5) * (1.0 / BLOCKS))
    code = (ocean_f * strip + (1.0 - ocean_f) * OCEAN) * BLOCKS + block_place(block - BLOCKS * strip) + 1.0
    code_high = jnp.floor(code * (1.0 / 32.0))
    code_low = code - 32.0 * code_high
    code_slot = slot_iota == jnp.where(active, tile_row * 8.0 + CAP, -1.0)
    lane_base = (lax.rem(tile, GROUP) * 8).astype(F32)
    spots = (iota((BLK, BLK), 1).astype(F32) == lane_base + order_col).astype(BF16)
    codes = 32.0 * dot(jnp.where(code_slot, code_high, 0.0).astype(BF16), spots) + dot(
        jnp.where(code_slot, code_low, 0.0).astype(BF16), spots
    )
    high, low = split(contrib[...])
    buckets = dot(place, high) + dot(place, low)
    buckets = jnp.concatenate([buckets[:, :BLK] + codes, buckets[:, BLK:]], axis=1)
    send[...] = buckets.reshape(TILES, 8, COUPLED * BLK)

    for copy in kappa_loads:
        copy.wait()
    mask_load.wait()
    row = iota((TALL, BLK), 0)
    beyond = ((row < HALO) & jnp.logical_not(has_down)) | ((row >= TOP) & jnp.logical_not(has_up))
    inside = jnp.where(beyond, 0.0, 1.0)
    for j in range(COLS):
        planes[SEA, j] = inside
        planes[SEA, j, pl.ds(HALO, BY), :] = jnp.maximum(
            mask_in[:, j * BLK : (j + 1) * BLK].astype(F32), 1.0 - ocean_f
        )

    sides_in = has_up.astype(jnp.int32) + has_down.astype(jnp.int32)
    pl.semaphore_wait(barrier, jnp.where(is_ocean, OCEAN * TILES + 2, TILES + 2 + 3 * sides_in))

    def remote(source, target, sems, n, device):
        return pltpu.make_async_remote_copy(
            src_ref=source,
            dst_ref=target,
            send_sem=sems.at[0, n],
            recv_sem=sems.at[1, n],
            device_id=device,
            device_id_type=MESH,
        )

    def row_copies(cut, sems, n):
        return [
            (has_up, has_down, remote(cut(TOP - HALO), cut(0), sems, n, (comp + 1, tile))),
            (has_down, has_up, remote(cut(HALO), cut(TOP), sems, n + 1, (comp - 1, tile))),
        ]

    def column_copies(source, target, sems, n):
        out = []
        for side, there in ((0, left), (1, right)):
            out += [
                (None, None, remote(source(side, HALO, BY), target(side, HALO, BY), sems, n, (comp, there))),
                (has_up, has_down, remote(
                    source(side, TOP - HALO, HALO), target(side, 0, HALO), sems, n + 1, (comp + 1, there))),
                (has_down, has_up, remote(
                    source(side, HALO, HALO), target(side, TOP, HALO), sems, n + 2, (comp - 1, there))),
            ]
            n += 3
        return out

    def each(copies, pick, act):
        for entry in copies:
            cond, copy = entry[pick], entry[2]
            if cond is None:
                act(copy)()
            else:
                pl.when(cond)(act(copy))

    def start(copies):
        each(copies, 0, lambda copy: copy.start)

    def wait_recv(copies):
        each(copies, 1, lambda copy: copy.wait_recv)

    def wait_send(copies):
        each(copies, 0, lambda copy: copy.wait_send)

    def plane_rows(first, number):
        return lambda y: planes.at[pl.ds(first, number), pl.ds(0, COLS), pl.ds(y, HALO), :]

    def plane_edge(first, number):
        return lambda side, y, rows: planes.at[pl.ds(first, number), side * (COLS - 1), pl.ds(y, rows), :]

    def side_edge(first, number):
        return lambda side, y, rows: sides.at[side, pl.ds(first, number), pl.ds(y, rows), :]

    early = row_copies(plane_rows(KAPPA, 1), row_sem, 0) + column_copies(
        plane_edge(KAPPA, 2), side_edge(KAPPA, 2), side_sem, 0
    )
    start(early)

    @pl.when(is_ocean)
    def _():
        def body(i, carry):
            t = lax.rem(i + tile, TILES)
            pltpu.make_async_remote_copy(
                src_ref=send.at[t, pl.ds(0, PAIR)],
                dst_ref=received.at[tile, pl.ds(0, PAIR)],
                send_sem=remap_send,
                recv_sem=remap_recv,
                device_id=(i // TILES, t),
                device_id_type=MESH,
            ).start()
            return carry

        lax.fori_loop(0, OCEAN * TILES, body, 0)

    @pl.when(jnp.logical_not(is_ocean))
    def _():
        def body(i, carry):
            t = lax.rem(i + tile, TILES)
            pltpu.make_async_remote_copy(
                src_ref=send.at[t, pl.ds(0, PAIR)],
                dst_ref=received.at[comp * TILES + tile, pl.ds(0, PAIR)],
                send_sem=remap_send,
                recv_sem=remap_recv,
                device_id=(OCEAN, t),
                device_id_type=MESH,
            ).start()
            return carry

        lax.fori_loop(0, TILES, body, 0)

    for copy in state_loads:
        copy.wait()
    flat = as_rows(natural)

    def turn(y):
        for j in range(HALF):
            parts = []
            for slab in (j, j + HALF):
                sea = planes[SEA, slab, pl.ds(HALO + y, 1), :] > 0.0
                for g in range(LANES // 8):
                    levels = flat[level_rows(slab, g, y), :]
                    parts.append(jnp.where(sea, levels, 0.0))
            field[HALO + y, pl.ds(FIRST + j * BLK, BLK), :] = jnp.concatenate(parts, axis=0).T

    def outer(i, carry):
        turn(jnp.where(i < HALO, i, i + BY - 2 * HALO))
        return carry

    def inner(i, carry):
        turn(i + HALO)
        return carry

    lax.fori_loop(0, 2 * HALO, outer, 0, unroll=4)
    deep_rows = row_copies(
        lambda y: field.at[pl.ds(y, HALO), pl.ds(FIRST, HALF * BLK), :], row_sem, 2
    )
    start(deep_rows)
    lax.fori_loop(0, BY - 2 * HALO, inner, 0, unroll=4)
    deep_sides = column_copies(
        lambda side, y, rows: field.at[pl.ds(y, rows), pl.ds(LAST - HALO if side else FIRST, HALO), :],
        lambda side, y, rows: ends.at[side, pl.ds(y, rows), pl.ds(HALO if side else 0, HALO), :],
        side_sem, 6,
    )
    start(deep_sides)

    wait_recv(early)
    lane = iota((TALL, BLK), 1)
    for side in range(2):
        sides[side, SEA, pl.ds(0, HALO), :] = inside[:HALO]
        sides[side, SEA, pl.ds(TOP, HALO), :] = inside[TOP:]
    for p in (KAPPA, SEA):
        planes[p, COLS] = jnp.where(lane < BLK // 2, sides[0, p], sides[1, p])
    sea = wide(planes, SEA)
    scale = jnp.where(sea > 0.0, wide(planes, KAPPA), 0.0)
    middle = 1.0 - scale * neighbours(sea)
    for n, value in enumerate((middle, scale)):
        tiles = [value[:, j * BLK : (j + 1) * BLK] for j in range(COLS + 1)]
        for j in range(COLS + 1):
            coef[n, j] = tiles[j]
        coef[n, COLS + 1] = jnp.where(lane < BLK // 2, tiles[HALF], tiles[COLS])
        coef[n, COLS + 2] = jnp.where(lane < BLK // 2, tiles[COLS], tiles[HALF - 1])

    def spread_row(y, carry):
        for n, target in enumerate((centre, around)):
            for a, b, at in [(j, j + HALF, FIRST + j * BLK) for j in range(HALF)] + [(COLS + 1, COLS + 2, None)]:
                both = jnp.concatenate(
                    [
                        jnp.broadcast_to(coef[n, a, pl.ds(y, 1), :], (LANES, BLK)),
                        jnp.broadcast_to(coef[n, b, pl.ds(y, 1), :], (LANES, BLK)),
                    ],
                    axis=0,
                ).T
                if at is None:
                    target[y, pl.ds(LAST, 8), :] = both[:8]
                    target[y, pl.ds(0, 8), :] = both[BLK - 8 :]
                else:
                    target[y, pl.ds(at, BLK), :] = both
        return carry

    lax.fori_loop(0, TALL, spread_row, 0, unroll=2)

    def join(y, carry):
        low = iota((8, BLK), 1) < LANES
        first = field[y, pl.ds(FIRST, 8), :]
        last = field[y, pl.ds(LAST - 8, 8), :]
        field[y, pl.ds(LAST, 8), :] = pltpu.roll(jnp.where(low, ends[0, y], first), LANES, 1)
        field[y, pl.ds(0, 8), :] = pltpu.roll(jnp.where(low, last, ends[1, y]), LANES, 1)
        return carry

    wait_recv(deep_sides)
    lax.fori_loop(HALO, TOP, join, 0, unroll=4)
    step_blocks(field, other, around, centre, 1, 10, 29, (1, 3))
    wait_recv(deep_rows)

    @pl.when(jnp.logical_not(has_down))
    def _():
        field[pl.ds(0, HALO)] = jnp.zeros((HALO, LONG, BLK), F32)

    @pl.when(jnp.logical_not(has_up))
    def _():
        field[pl.ds(TOP, HALO)] = jnp.zeros((HALO, LONG, BLK), F32)

    @pl.when(has_down)
    def _():
        lax.fori_loop(0, HALO, join, 0, unroll=4)

    @pl.when(has_up)
    def _():
        lax.fori_loop(TOP, TALL, join, 0, unroll=4)

    step_blocks(field, other, around, centre, 1, 10, 29, (0, 1))
    step_blocks(field, other, around, centre, 1, 10, 29, (3, 4))
    wait_send(deep_rows)
    wait_send(deep_sides)
    step_blocks(other, field, around, centre, 2, 9, 29, (0, 4))

    def accumulate(sources):
        whole = received.at[pl.ds(0, sources), pl.ds(0, PAIR)]
        pltpu.make_async_copy(whole, whole, remap_recv).wait()
        heads = received[pl.ds(0, sources), CAP, :BLK]
        offset = 1.0 + BLOCKS * comp.astype(F32)
        total = jnp.zeros((BLOCKS, COUPLED * BLK), F32)
        for g in range(sources // GROUP):
            codes_in = jnp.sum(heads[GROUP * g : GROUP * g + GROUP], axis=0, keepdims=True) - offset
            codes_in = codes_in[:, : GROUP * 8]
            onehot = (iota((BLOCKS, GROUP * 8), 0).astype(F32) == codes_in).astype(BF16)
            values = received[pl.ds(GROUP * g, GROUP)].reshape(GROUP * 8, COUPLED * BLK)
            big, little = split(values)
            total = total + dot(onehot, big) + dot(onehot, little)
        for j in range(COLS):
            weight_here = 0.5 * mask_in[:, j * BLK : (j + 1) * BLK].astype(F32)
            for f in range(COUPLED):
                old = own(planes, f, j)
                new = total[j * BY : (j + 1) * BY, f * BLK : (f + 1) * BLK]
                planes[f, j, pl.ds(HALO, BY), :] = old + weight_here * (new - old)

    pl.when(is_ocean)(lambda: accumulate(OCEAN * TILES))
    pl.when(jnp.logical_not(is_ocean))(lambda: accumulate(TILES))

    late = row_copies(plane_rows(0, COUPLED), row_sem, 4) + column_copies(
        plane_edge(0, COUPLED), side_edge(0, COUPLED), side_sem, 12
    )
    start(late)
    step_blocks(field, other, around, centre, 3, 9, 28, (0, 4))
    wait_recv(late)

    wait_send(early)
    wait_send(late)

    @pl.when(is_ocean)
    def _():
        whole = received.at[:, pl.ds(0, PAIR)]
        pltpu.make_async_copy(whole, whole, remap_send).wait()

    @pl.when(jnp.logical_not(is_ocean))
    def _():
        whole = received.at[pl.ds(0, TILES), pl.ds(0, PAIR)]
        pltpu.make_async_copy(whole, whole, remap_send).wait()

    step_blocks(other, field, around, centre, HALO, 8, 28, (0, 4))


def finish_kernel(natural, planes, sides, coef, field, out, result, done, sem):
    flat, flat_result = as_rows(natural), as_rows(result)
    copies = []
    for j in range(HALF):

        def turn(y, carry, j=j):
            back = field[HALO + y, pl.ds(FIRST + j * BLK, BLK), :].T
            for h, slab in enumerate((j, j + HALF)):
                sea = planes[SEA, slab, pl.ds(HALO + y, 1), :] > 0.0
                for g in range(LANES // 8):
                    at = level_rows(slab, g, y)
                    piece = back[h * LANES + g * 8 : h * LANES + g * 8 + 8]
                    flat_result[at, :] = jnp.where(sea, piece, flat[at, :])
            return carry

        lax.fori_loop(0, BY, turn, 0, unroll=8)
        for slab in (j, j + HALF):
            copies.append(
                pltpu.make_async_copy(
                    result.at[slab, pl.ds(0, DEEP), pl.ds(0, BY), :],
                    out.at[pl.ds(COUPLED, DEEP), :, pl.ds(slab * BLK, BLK)],
                    sem.at[slab],
                )
            )
            copies[-1].start()

    lane = iota((TALL, BLK), 1)
    sea = wide(planes, SEA) > 0.0
    middle, scale = wide(coef, 0), wide(coef, 1)
    for f in range(COUPLED):
        edge = jnp.where(lane < BLK // 2, sides[0, f], sides[1, f])
        v = jnp.concatenate([planes[f, j] for j in range(COLS)] + [edge], axis=1)
        w = jnp.where(sea, v, 0.0)
        for _ in range(4):
            w = middle * w + scale * neighbours(w)
        done[f] = jnp.where(sea, w, v)[HALO:TOP, :BX]
    copies.append(pltpu.make_async_copy(done, out.at[pl.ds(0, COUPLED)], sem.at[COLS]))
    copies[-1].start()
    for copy in copies:
        copy.wait()


def shards(state, kappa, land_mask, remap_weight, remap_src, remap_tile, remap_block, remap_count):
    vmem = pl.BlockSpec(memory_space=pltpu.VMEM)
    hbm = pl.BlockSpec(memory_space=pltpu.HBM)
    kept = (
        pltpu.VMEM((COLS, LANES, TALL, BLK), F32),
        pltpu.VMEM((5, COLS + 1, TALL, BLK), F32),
        pltpu.VMEM((2, 5, TALL, BLK), F32),
        pltpu.VMEM((2, COLS + 3, TALL, BLK), F32),
        pltpu.VMEM((TALL, LONG, BLK), F32),
    )
    operands = (
        state, kappa, land_mask, remap_weight,
        remap_src.reshape(1, SLOTS), remap_tile.reshape(1, SLOTS),
        remap_block.reshape(1, SLOTS),
    )
    dma = pltpu.SemaphoreType.DMA
    natural, planes, sides, coef, field = pl.pallas_call(
        exchange_kernel,
        out_shape=kept,
        in_specs=[hbm] * 7 + [pl.BlockSpec(memory_space=pltpu.SMEM)],
        out_specs=(vmem,) * len(kept),
        scratch_shapes=[
            pltpu.VMEM((TALL, LONG, BLK), F32),
            pltpu.VMEM((TALL, LONG, BLK), F32),
            pltpu.VMEM((TALL, LONG, BLK), F32),
            pltpu.VMEM((2, TALL, 8, BLK), F32),
            pltpu.VMEM((SLOTS, BLK, BLK), BF16),
            pltpu.VMEM((BY, BX), jnp.int32),
            pltpu.VMEM((3, 1, SLOTS), jnp.int32),
            pltpu.VMEM((TILES, 8, COUPLED * BLK), F32),
            pltpu.VMEM((OCEAN * TILES, 8, COUPLED * BLK), F32),
            pltpu.VMEM((SLOTS, COUPLED * BLK), F32),
            dma((17,)),
            dma((WEIGHT_CHUNKS,)),
            dma((COLS,)),
            dma,
            dma,
            dma((2, 6)),
            dma((2, 18)),
        ],
        compiler_params=pltpu.CompilerParams(
            collective_id=0, has_side_effects=True, vmem_limit_bytes=36 << 20
        ),
        name="exchange",
    )(*(pltpu.with_memory_space_constraint(x, pltpu.HBM) for x in operands), remap_count)
    return pl.pallas_call(
        finish_kernel,
        out_shape=jax.ShapeDtypeStruct((LEVELS, BY, BX), F32),
        in_specs=[vmem] * len(kept),
        out_specs=hbm,
        scratch_shapes=[pltpu.VMEM((COLS, LANES, TALL, BLK), F32), pltpu.VMEM((COUPLED, BY, BX), F32), dma((COLS + 1,))],
        compiler_params=pltpu.CompilerParams(vmem_limit_bytes=16 << 20),
        name="finish",
    )(natural, planes, sides, coef, field)


def solution(mesh):
    return jax.shard_map(
        shards,
        mesh=mesh,
        in_specs=(
            P(None, "comp", "tile"),
            P("comp", "tile"),
            P("comp", "tile"),
            P(("comp", "tile"), None, None),
            P(("comp", "tile")),
            P(("comp", "tile"), None),
            P(("comp", "tile")),
            P(("comp", "tile")),
        ),
        out_specs=P(None, "comp", "tile"),
        check_vma=False,
    )
```

profile of v0, /device:TPU:1, one launch (start us, length us, event | category | flops | bytes accessed | tf_op | source)
XLA Modules:
  0.0 50.2 jit_solution(12003617118490552410)
XLA Ops:
  0.7 44.7 %exchange.1 = (f32[6,64,40,128]{3,2,1,0:T(8,128)S(1)}, f32[5,7,40,128]{3,2,1,0:T(8,128)S(1)}, f32[2,5,40,128]{3,2,1,0:T(8,128)S(1)}, f32[2,9,40,128]{3,2,1,0:T(8,128)S(1)}, f32[40,400,128]{2,1,0:T(8,128)S(1)}) custom-call(f32[60,32,768]{2,1,0:T(8,128)} %state.1, f32[32,768]{1,0:T(8,128)} %kappa.1, s32[32,768]{1,0:T(8,128)} %mask.1, ...), custom_call_target="tpu_custom_call" | custom-call | tf_op jit(solution)/shard_map/exchange/pallas_call | solution.py:569
  45.3 4.8 %finish.1 = f32[60,32,768]{2,1,0:T(8,128)} custom-call(f32[6,64,40,128]{3,2,1,0:T(8,128)S(1)} %get-tuple-element.10.natural, f32[5,7,40,128]{3,2,1,0:T(8,128)S(1)} %get-tuple-element.11.planes, f32[2,5,40,128]{3,2,1,0:T(8,128)S(1)} %get-tuple-element.12.sides, f32[2,9,40,128]{3,2,1,0:T(8,128)S(1)} %get-tuple-element.13.coef, ...), custom_call_target="tpu_custom_call" | custom-call | tf_op jit(solution)/shard_map/finish/pallas_call | solution.py:598
where the time goes:
time: 50.3 us; the launch traced here: 50.2 us
  Pallas kernels  49.5 us (98%)
  between operations  0.66 us (1%)
    pallas_call x1, Pallas kernels, shards(): pl.pallas_call(exchange_kernel, out_shape=kept, in_specs=[hbm] * 7 + [pl....  44.7 us
    pallas_call x1, Pallas kernels, shards(): pl.pallas_call(finish_kernel, out_shape=jax.ShapeDtypeStruct((LEVELS, BY,...  4.82 us

commit v1 on v0

--- a/solution.py
+++ b/solution.py
@@ -107,13 +107,21 @@
         step_rows(old, new, around, centre, jnp.minimum(start + count * b, last), count)
         return carry
 
-    lax.fori_loop(*blocks, one, 0)
+    lax.fori_loop(0, blocks, one, 0)
+
+
+def step_outer(old, new, around, centre, start):
+    def one(b, carry):
+        step_rows(old, new, around, centre, start + b * (TOP - 2 * start), HALO)
+        return carry
+
+    lax.fori_loop(0, 2, one, 0)
 
 
 def exchange_kernel(
     state, kappa, mask, weight, src, tile_of, block_of, count,
-    natural, planes, sides, coef, field, around, centre,
-    other, ends, weights, mask_in, small, send, received, contrib,
+    natural, planes, sides, coef,
+    field, around, centre, other, ends, weights, mask_in, small, send, received, contrib,
     load_sem, weight_sem, state_sem, remap_send, remap_recv, row_sem, side_sem,
 ):
     comp = lax.axis_index("comp")
@@ -156,7 +164,7 @@
         pltpu.make_async_copy(weight.at[pl.ds(n * per, per)], weights.at[pl.ds(n * per, per)], weight_sem.at[n])
         for n in range(WEIGHT_CHUNKS)
     ]
-    for copy in loads + surface_loads + weight_loads + kappa_loads + [mask_load] + state_loads:
+    for copy in loads + kappa_loads + [mask_load] + state_loads + surface_loads + weight_loads:
         copy.start()
 
     barrier = pltpu.get_barrier_semaphore()
@@ -194,6 +202,137 @@
         lax.fori_loop(0, TILES, body, 0)
 
     received[:, PAIR:, :] = jnp.zeros((received.shape[0], 8 - PAIR, received.shape[2]), F32)
+
+    ocean_f = jnp.where(is_ocean, 1.0, 0.0)
+
+    for copy in kappa_loads:
+        copy.wait()
+    mask_load.wait()
+    row = iota((TALL, BLK), 0)
+    beyond = ((row < HALO) & jnp.logical_not(has_down)) | ((row >= TOP) & jnp.logical_not(has_up))
+    inside = jnp.where(beyond, 0.0, 1.0)
+    for j in range(COLS):
+        planes[SEA, j] = inside
+        planes[SEA, j, pl.ds(HALO, BY), :] = jnp.maximum(
+            mask_in[:, j * BLK : (j + 1) * BLK].astype(F32), 1.0 - ocean_f
+        )
+
+    sides_in = has_up.astype(jnp.int32) + has_down.astype(jnp.int32)
+    pl.semaphore_wait(barrier, jnp.where(is_ocean, OCEAN * TILES + 2, TILES + 2 + 3 * sides_in))
+
+    def remote(source, target, sems, n, device):
+        return pltpu.make_async_remote_copy(
+            src_ref=source,
+            dst_ref=target,
+            send_sem=sems.at[0, n],
+            recv_sem=sems.at[1, n],
+            device_id=device,
+            device_id_type=MESH,
+        )
+
+    def row_copies(cut, sems, n):
+        return [
+            (has_up, has_down, remote(cut(TOP - HALO), cut(0), sems, n, (comp + 1, tile))),
+            (has_down, has_up, remote(cut(HALO), cut(TOP), sems, n + 1, (comp - 1, tile))),
+        ]
+
+    def column_copies(source, target, sems, n):
+        out = []
+        for side, there in ((0, left), (1, right)):
+            out += [
+                (None, None, remote(source(side, HALO, BY), target(side, HALO, BY), sems, n, (comp, there))),
+                (has_up, has_down, remote(
+                    source(side, TOP - HALO, HALO), target(side, 0, HALO), sems, n + 1, (comp + 1, there))),
+                (has_down, has_up, remote(
+                    source(side, HALO, HALO), target(side, TOP, HALO), sems, n + 2, (comp - 1, there))),
+            ]
+            n += 3
+        return out
+
+    def each(copies, pick, act):
+        for entry in copies:
+            cond, copy = entry[pick], entry[2]
+            if cond is None:
+                act(copy)()
+            else:
+                pl.when(cond)(act(copy))
+
+    def start(copies):
+        each(copies, 0, lambda copy: copy.start)
+
+    def wait_recv(copies):
+        each(copies, 1, lambda copy: copy.wait_recv)
+
+    def wait_send(copies):
+        each(copies, 0, lambda copy: copy.wait_send)
+
+    def plane_rows(first, number):
+        return lambda y: planes.at[pl.ds(first, number), pl.ds(0, COLS), pl.ds(y, HALO), :]
+
+    def plane_edge(first, number):
+        return lambda side, y, rows: planes.at[pl.ds(first, number), side * (COLS - 1), pl.ds(y, rows), :]
+
+    def side_edge(first, number):
+        return lambda side, y, rows: sides.at[side, pl.ds(first, number), pl.ds(y, rows), :]
+
+    early = row_copies(plane_rows(KAPPA, 1), row_sem, 0) + column_copies(
+        plane_edge(KAPPA, 2), side_edge(KAPPA, 2), side_sem, 0
+    )
+    start(early)
+
+    deep_rows = []
+    for j in range(COLS):
+        for up, down, base, at, there, n in (
+            (has_up, has_down, BY - HALO, BY, comp + 1, 4 + j),
+            (has_down, has_up, 0, TOP, comp - 1, 4 + COLS + j),
+        ):
+            deep_rows.append((up, down, remote(
+                state.at[pl.ds(COUPLED, DEEP), pl.ds(base, HALO), pl.ds(j * BLK, BLK)],
+                natural.at[j, pl.ds(0, DEEP), pl.ds(at, HALO), :],
+                row_sem, n, (there, tile),
+            )))
+    start(deep_rows[:COLS])
+
+    for copy in state_loads:
+        copy.wait()
+    flat = as_rows(natural)
+
+    def turn(source, target):
+        for j in range(HALF):
+            parts = []
+            for slab in (j, j + HALF):
+                sea = planes[SEA, slab, pl.ds(target, 1), :] > 0.0
+                for g in range(LANES // 8):
+                    parts.append(jnp.where(sea, flat[level_rows(slab, g, source), :], 0.0))
+            field[target, pl.ds(FIRST + j * BLK, BLK), :] = jnp.concatenate(parts, axis=0).T
+
+    def turn_rows(source, target, number):
+        def one(i, carry):
+            turn(source + i, target + i)
+            return carry
+
+        lax.fori_loop(0, number, one, 0, unroll=4)
+
+    def turn_back(y, carry):
+        for j in range(HALF):
+            back = field[HALO + y, pl.ds(FIRST + j * BLK, BLK), :].T
+            for h, slab in enumerate((j, j + HALF)):
+                sea = planes[SEA, slab, pl.ds(HALO + y, 1), :] > 0.0
+                for g in range(LANES // 8):
+                    at = level_rows(slab, g, y)
+                    piece = back[h * LANES + g * 8 : h * LANES + g * 8 + 8]
+                    flat[at, :] = jnp.where(sea, piece, flat[at, :])
+        return carry
+
+    turn_rows(0, HALO, BY)
+    deep_sides = column_copies(
+        lambda side, y, rows: field.at[pl.ds(y, rows), pl.ds(LAST - HALO if side else FIRST, HALO), :],
+        lambda side, y, rows: ends.at[side, pl.ds(y, rows), pl.ds(HALO if side else 0, HALO), :],
+        side_sem, 6,
+    )
+    start(deep_sides)
+
+    start(deep_rows[COLS:])
 
     for copy in loads + surface_loads:
         copy.wait()
@@ -209,21 +348,6 @@
     src_place = to_column(block_place(small[0].astype(F32)))
     gather = (iota((BLK, 256), 1).astype(F32) == src_place).astype(BF16)
     picked_all = dot(gather, surface)
-    sub = iota((32, BLK), 0) % 8
-    for n in range(WEIGHT_CHUNKS):
-        weight_loads[n].wait()
-        for g in range(per // 8):
-            base = n * per + g * 8
-            picked = picked_all[base : base + 8]
-            lhs = jnp.concatenate(
-                [picked[:, f * BLK : (f + 1) * BLK] for f in range(COUPLED)] + [jnp.zeros((8, BLK), F32)], axis=0
-            )
-            spread = jnp.concatenate([jnp.where(sub == k, lhs, 0.0) for k in range(8)], axis=1).astype(BF16)
-            product = dot(spread, weights[pl.ds(base, 8)].reshape(8 * BLK, BLK))
-            for f in range(COUPLED):
-                contrib[pl.ds(base, 8), f * BLK : (f + 1) * BLK] = product[8 * f : 8 * f + 8]
-
-    ocean_f = jnp.where(is_ocean, 1.0, 0.0)
     active = iota((1, BLK), 1) < count[0]
     tile_row = small[1].astype(F32)
     tile_col = to_column(tile_row)
@@ -244,85 +368,24 @@
     codes = 32.0 * dot(jnp.where(code_slot, code_high, 0.0).astype(BF16), spots) + dot(
         jnp.where(code_slot, code_low, 0.0).astype(BF16), spots
     )
+    sub = iota((32, BLK), 0) % 8
+    for n in range(WEIGHT_CHUNKS):
+        weight_loads[n].wait()
+        for g in range(per // 8):
+            base = n * per + g * 8
+            picked = picked_all[base : base + 8]
+            lhs = jnp.concatenate(
+                [picked[:, f * BLK : (f + 1) * BLK] for f in range(COUPLED)] + [jnp.zeros((8, BLK), F32)], axis=0
+            )
+            spread = jnp.concatenate([jnp.where(sub == k, lhs, 0.0) for k in range(8)], axis=1).astype(BF16)
+            product = dot(spread, weights[pl.ds(base, 8)].reshape(8 * BLK, BLK))
+            for f in range(COUPLED):
+                contrib[pl.ds(base, 8), f * BLK : (f + 1) * BLK] = product[8 * f : 8 * f + 8]
+
     high, low = split(contrib[...])
     buckets = dot(place, high) + dot(place, low)
     buckets = jnp.concatenate([buckets[:, :BLK] + codes, buckets[:, BLK:]], axis=1)
     send[...] = buckets.reshape(TILES, 8, COUPLED * BLK)
-
-    for copy in kappa_loads:
-        copy.wait()
-    mask_load.wait()
-    row = iota((TALL, BLK), 0)
-    beyond = ((row < HALO) & jnp.logical_not(has_down)) | ((row >= TOP) & jnp.logical_not(has_up))
-    inside = jnp.where(beyond, 0.0, 1.0)
-    for j in range(COLS):
-        planes[SEA, j] = inside
-        planes[SEA, j, pl.ds(HALO, BY), :] = jnp.maximum(
-            mask_in[:, j * BLK : (j + 1) * BLK].astype(F32), 1.0 - ocean_f
-        )
-
-    sides_in = has_up.astype(jnp.int32) + has_down.astype(jnp.int32)
-    pl.semaphore_wait(barrier, jnp.where(is_ocean, OCEAN * TILES + 2, TILES + 2 + 3 * sides_in))
-
-    def remote(source, target, sems, n, device):
-        return pltpu.make_async_remote_copy(
-            src_ref=source,
-            dst_ref=target,
-            send_sem=sems.at[0, n],
-            recv_sem=sems.at[1, n],
-            device_id=device,
-            device_id_type=MESH,
-        )
-
-    def row_copies(cut, sems, n):
-        return [
-            (has_up, has_down, remote(cut(TOP - HALO), cut(0), sems, n, (comp + 1, tile))),
-            (has_down, has_up, remote(cut(HALO), cut(TOP), sems, n + 1, (comp - 1, tile))),
-        ]
-
-    def column_copies(source, target, sems, n):
-        out = []
-        for side, there in ((0, left), (1, right)):
-            out += [
-                (None, None, remote(source(side, HALO, BY), target(side, HALO, BY), sems, n, (comp, there))),
-                (has_up, has_down, remote(
-                    source(side, TOP - HALO, HALO), target(side, 0, HALO), sems, n + 1, (comp + 1, there))),
-                (has_down, has_up, remote(
-                    source(side, HALO, HALO), target(side, TOP, HALO), sems, n + 2, (comp - 1, there))),
-            ]
-            n += 3
-        return out
-
-    def each(copies, pick, act):
-        for entry in copies:
-            cond, copy = entry[pick], entry[2]
-            if cond is None:
-                act(copy)()
-            else:
-                pl.when(cond)(act(copy))
-
-    def start(copies):
-        each(copies, 0, lambda copy: copy.start)
-
-    def wait_recv(copies):
-        each(copies, 1, lambda copy: copy.wait_recv)
-
-    def wait_send(copies):
-        each(copies, 0, lambda copy: copy.wait_send)
-
-    def plane_rows(first, number):
-        return lambda y: planes.at[pl.ds(first, number), pl.ds(0, COLS), pl.ds(y, HALO), :]
-
-    def plane_edge(first, number):
-        return lambda side, y, rows: planes.at[pl.ds(first, number), side * (COLS - 1), pl.ds(y, rows), :]
-
-    def side_edge(first, number):
-        return lambda side, y, rows: sides.at[side, pl.ds(first, number), pl.ds(y, rows), :]
-
-    early = row_copies(plane_rows(KAPPA, 1), row_sem, 0) + column_copies(
-        plane_edge(KAPPA, 2), side_edge(KAPPA, 2), side_sem, 0
-    )
-    start(early)
 
     @pl.when(is_ocean)
     def _():
@@ -355,41 +418,6 @@
             return carry
 
         lax.fori_loop(0, TILES, body, 0)
-
-    for copy in state_loads:
-        copy.wait()
-    flat = as_rows(natural)
-
-    def turn(y):
-        for j in range(HALF):
-            parts = []
-            for slab in (j, j + HALF):
-                sea = planes[SEA, slab, pl.ds(HALO + y, 1), :] > 0.0
-                for g in range(LANES // 8):
-                    levels = flat[level_rows(slab, g, y), :]
-                    parts.append(jnp.where(sea, levels, 0.0))
-            field[HALO + y, pl.ds(FIRST + j * BLK, BLK), :] = jnp.concatenate(parts, axis=0).T
-
-    def outer(i, carry):
-        turn(jnp.where(i < HALO, i, i + BY - 2 * HALO))
-        return carry
-
-    def inner(i, carry):
-        turn(i + HALO)
-        return carry
-
-    lax.fori_loop(0, 2 * HALO, outer, 0, unroll=4)
-    deep_rows = row_copies(
-        lambda y: field.at[pl.ds(y, HALO), pl.ds(FIRST, HALF * BLK), :], row_sem, 2
-    )
-    start(deep_rows)
-    lax.fori_loop(0, BY - 2 * HALO, inner, 0, unroll=4)
-    deep_sides = column_copies(
-        lambda side, y, rows: field.at[pl.ds(y, rows), pl.ds(LAST - HALO if side else FIRST, HALO), :],
-        lambda side, y, rows: ends.at[side, pl.ds(y, rows), pl.ds(HALO if side else 0, HALO), :],
-        side_sem, 6,
-    )
-    start(deep_sides)
 
     wait_recv(early)
     lane = iota((TALL, BLK), 1)
@@ -437,30 +465,12 @@
 
     wait_recv(deep_sides)
     lax.fori_loop(HALO, TOP, join, 0, unroll=4)
-    step_blocks(field, other, around, centre, 1, 10, 29, (1, 3))
-    wait_recv(deep_rows)
-
-    @pl.when(jnp.logical_not(has_down))
-    def _():
-        field[pl.ds(0, HALO)] = jnp.zeros((HALO, LONG, BLK), F32)
-
-    @pl.when(jnp.logical_not(has_up))
-    def _():
-        field[pl.ds(TOP, HALO)] = jnp.zeros((HALO, LONG, BLK), F32)
-
-    @pl.when(has_down)
-    def _():
-        lax.fori_loop(0, HALO, join, 0, unroll=4)
-
-    @pl.when(has_up)
-    def _():
-        lax.fori_loop(TOP, TALL, join, 0, unroll=4)
-
-    step_blocks(field, other, around, centre, 1, 10, 29, (0, 1))
-    step_blocks(field, other, around, centre, 1, 10, 29, (3, 4))
-    wait_send(deep_rows)
+    step_blocks(field, other, around, centre, 5, 10, 25, 3)
     wait_send(deep_sides)
-    step_blocks(other, field, around, centre, 2, 9, 29, (0, 4))
+    step_blocks(other, field, around, centre, 6, 7, 27, 4)
+    step_blocks(field, other, around, centre, 7, 9, 24, 3)
+    step_blocks(other, field, around, centre, 8, 8, 24, 3)
+    lax.fori_loop(HALO, BY - HALO, turn_back, 0, unroll=4)
 
     def accumulate(sources):
         whole = received.at[pl.ds(0, sources), pl.ds(0, PAIR)]
@@ -485,15 +495,45 @@
     pl.when(is_ocean)(lambda: accumulate(OCEAN * TILES))
     pl.when(jnp.logical_not(is_ocean))(lambda: accumulate(TILES))
 
-    late = row_copies(plane_rows(0, COUPLED), row_sem, 4) + column_copies(
+    late = row_copies(plane_rows(0, COUPLED), row_sem, 2) + column_copies(
         plane_edge(0, COUPLED), side_edge(0, COUPLED), side_sem, 12
     )
     start(late)
-    step_blocks(field, other, around, centre, 3, 9, 28, (0, 4))
+
+    wait_recv(deep_rows)
+
+    @pl.when(has_down)
+    def _():
+        turn_rows(BY, 0, HALO)
+        lax.fori_loop(0, HALO, join, 0, unroll=4)
+
+    @pl.when(has_up)
+    def _():
+        turn_rows(TOP, TOP, HALO)
+        lax.fori_loop(TOP, TALL, join, 0, unroll=4)
+
+    @pl.when(jnp.logical_not(has_down))
+    def _():
+        field[pl.ds(0, HALO)] = jnp.zeros((HALO, LONG, BLK), F32)
+
+    @pl.when(jnp.logical_not(has_up))
+    def _():
+        field[pl.ds(TOP, HALO)] = jnp.zeros((HALO, LONG, BLK), F32)
+
+    step_outer(field, other, around, centre, 1)
+    step_outer(other, field, around, centre, 2)
+    step_outer(field, other, around, centre, 3)
+    step_outer(other, field, around, centre, 4)
+
+    def turn_back_outer(i, carry):
+        return turn_back(jnp.where(i < HALO, i, i + BY - 2 * HALO), carry)
+
+    lax.fori_loop(0, 2 * HALO, turn_back_outer, 0, unroll=4)
     wait_recv(late)
 
     wait_send(early)
     wait_send(late)
+    wait_send(deep_rows)
 
     @pl.when(is_ocean)
     def _():
@@ -505,35 +545,18 @@
         whole = received.at[pl.ds(0, TILES), pl.ds(0, PAIR)]
         pltpu.make_async_copy(whole, whole, remap_send).wait()
 
-    step_blocks(other, field, around, centre, HALO, 8, 28, (0, 4))
-
-
-def finish_kernel(natural, planes, sides, coef, field, out, result, done, sem):
-    flat, flat_result = as_rows(natural), as_rows(result)
-    copies = []
-    for j in range(HALF):
-
-        def turn(y, carry, j=j):
-            back = field[HALO + y, pl.ds(FIRST + j * BLK, BLK), :].T
-            for h, slab in enumerate((j, j + HALF)):
-                sea = planes[SEA, slab, pl.ds(HALO + y, 1), :] > 0.0
-                for g in range(LANES // 8):
-                    at = level_rows(slab, g, y)
-                    piece = back[h * LANES + g * 8 : h * LANES + g * 8 + 8]
-                    flat_result[at, :] = jnp.where(sea, piece, flat[at, :])
-            return carry
-
-        lax.fori_loop(0, BY, turn, 0, unroll=8)
-        for slab in (j, j + HALF):
-            copies.append(
-                pltpu.make_async_copy(
-                    result.at[slab, pl.ds(0, DEEP), pl.ds(0, BY), :],
-                    out.at[pl.ds(COUPLED, DEEP), :, pl.ds(slab * BLK, BLK)],
-                    sem.at[slab],
-                )
-            )
-            copies[-1].start()
-
+
+def finish_kernel(natural, planes, sides, coef, out, done, sem):
+    copies = [
+        pltpu.make_async_copy(
+            natural.at[j, pl.ds(0, DEEP), pl.ds(0, BY), :],
+            out.at[pl.ds(COUPLED, DEEP), :, pl.ds(j * BLK, BLK)],
+            sem.at[j],
+        )
+        for j in range(COLS)
+    ]
+    for copy in copies:
+        copy.start()
     lane = iota((TALL, BLK), 1)
     sea = wide(planes, SEA) > 0.0
     middle, scale = wide(coef, 0), wide(coef, 1)
@@ -558,7 +581,6 @@
         pltpu.VMEM((5, COLS + 1, TALL, BLK), F32),
         pltpu.VMEM((2, 5, TALL, BLK), F32),
         pltpu.VMEM((2, COLS + 3, TALL, BLK), F32),
-        pltpu.VMEM((TALL, LONG, BLK), F32),
     )
     operands = (
         state, kappa, land_mask, remap_weight,
@@ -566,12 +588,13 @@
         remap_block.reshape(1, SLOTS),
     )
     dma = pltpu.SemaphoreType.DMA
-    natural, planes, sides, coef, field = pl.pallas_call(
+    natural, planes, sides, coef = pl.pallas_call(
         exchange_kernel,
         out_shape=kept,
         in_specs=[hbm] * 7 + [pl.BlockSpec(memory_space=pltpu.SMEM)],
         out_specs=(vmem,) * len(kept),
         scratch_shapes=[
+            pltpu.VMEM((TALL, LONG, BLK), F32),
             pltpu.VMEM((TALL, LONG, BLK), F32),
             pltpu.VMEM((TALL, LONG, BLK), F32),
             pltpu.VMEM((TALL, LONG, BLK), F32),
@@ -587,11 +610,11 @@
             dma((COLS,)),
             dma,
             dma,
-            dma((2, 6)),
+            dma((2, 4 + 2 * COLS)),
             dma((2, 18)),
         ],
         compiler_params=pltpu.CompilerParams(
-            collective_id=0, has_side_effects=True, vmem_limit_bytes=36 << 20
+            collective_id=0, has_side_effects=True, vmem_limit_bytes=44 << 20
         ),
         name="exchange",
     )(*(pltpu.with_memory_space_constraint(x, pltpu.HBM) for x in operands), remap_count)
@@ -600,10 +623,10 @@
         out_shape=jax.ShapeDtypeStruct((LEVELS, BY, BX), F32),
         in_specs=[vmem] * len(kept),
         out_specs=hbm,
-        scratch_shapes=[pltpu.VMEM((COLS, LANES, TALL, BLK), F32), pltpu.VMEM((COUPLED, BY, BX), F32), dma((COLS + 1,))],
+        scratch_shapes=[pltpu.VMEM((COUPLED, BY, BX), F32), dma((COLS + 1,))],
         compiler_params=pltpu.CompilerParams(vmem_limit_bytes=16 << 20),
         name="finish",
-    )(natural, planes, sides, coef, field)
+    )(natural, planes, sides, coef)
 
 
 def solution(mesh):

time: 50.3 us -> 41.2 us (0.82)
  Pallas kernels: 49.5 us -> 40.5 us
    pallas_call x1, Pallas kernels: 44.7 us -> 37.9 us  [shards(): pl.pallas_call(exchange_kernel, out_shape=kept, in_specs=[hbm] * 7 + [pl....]
    pallas_call x1, Pallas kernels: 4.82 us -> 2.6 us  [shards(): pl.pallas_call(finish_kernel, out_shape=jax.ShapeDtypeStruct((LEVELS, BY,...]
where the time goes in v1:
time: 41.2 us; the launch traced here: 41.1 us
  Pallas kernels  40.5 us (98%)
  between operations  0.66 us (2%)
    pallas_call x1, Pallas kernels, shards(): pl.pallas_call(exchange_kernel, out_shape=kept, in_specs=[hbm] * 7 + [pl....  37.9 us
    pallas_call x1, Pallas kernels, shards(): pl.pallas_call(finish_kernel, out_shape=jax.ShapeDtypeStruct((LEVELS, BY,...  2.6 us

profile of v1, /device:TPU:1, one launch (start us, length us, event | category | flops | bytes accessed | tf_op | source)
XLA Modules:
  0.0 41.1 jit_solution(14745875711050390760)
XLA Ops:
  0.7 37.9 %exchange.1 = (f32[6,64,40,128]{3,2,1,0:T(8,128)S(1)}, f32[5,7,40,128]{3,2,1,0:T(8,128)S(1)}, f32[2,5,40,128]{3,2,1,0:T(8,128)S(1)}, f32[2,9,40,128]{3,2,1,0:T(8,128)S(1)}) custom-call(f32[60,32,768]{2,1,0:T(8,128)} %state.1, f32[32,768]{1,0:T(8,128)} %kappa.1, s32[32,768]{1,0:T(8,128)} %mask.1, bf16[128,128,128]{2,1,0:T(8,128)(2,1)} %weight.1, ...), custom_call_target="tpu_custom_call" | custom-call | tf_op jit(solution)/shard_map/exchange/pallas_call | solution.py:591
  38.5 2.6 %finish.1 = f32[60,32,768]{2,1,0:T(8,128)} custom-call(f32[6,64,40,128]{3,2,1,0:T(8,128)S(1)} %get-tuple-element.9.natural, f32[5,7,40,128]{3,2,1,0:T(8,128)S(1)} %get-tuple-element.10.planes, f32[2,5,40,128]{3,2,1,0:T(8,128)S(1)} %get-tuple-element.11.sides, f32[2,9,40,128]{3,2,1,0:T(8,128)S(1)} %get-tuple-element.12.coef), custom_call_target="tpu_custom_call" | custom-call | tf_op jit(solution)/shard_map/finish/pallas_call | solution.py:621

commit v2 on v1

--- a/solution.py
+++ b/solution.py
@@ -30,7 +30,10 @@
 LONG = LAST + 8
 STRIDE = 49
 WEIGHT_CHUNKS = 4
+PART = 12
+SLABS = 1
 GROUP = min(16, TILES)
+PASSED = TILES // 2
 MESH = pl.DeviceIdType.MESH
 F32 = jnp.float32
 BF16 = jnp.bfloat16
@@ -82,6 +85,8 @@
 
 
 def step_rows(old, new, around, centre, y0, count):
+    faces = None if not callable(centre) else [centre(y0 + y) for y in range(count)]
+
     def load(ref, y, i):
         return ref[y0 + y, pl.ds(HALO + i, 8, stride=STRIDE), :]
 
@@ -91,9 +96,11 @@
         diagonal = [here[y] + ahead[y + 1] for y in range(count + 1)]
         for y in range(count):
             near = before[y] + diagonal[y]
-            new[y0 + y, pl.ds(HALO + i, 8, stride=STRIDE), :] = (
-                load(centre, y, i) * here[y + 1] + load(around, y, i) * near
-            )
+            if faces is None:
+                value = load(centre, y, i) * here[y + 1] + load(around, y, i) * near
+            else:
+                value = here[y + 1] + load(around, y, i) * (near - faces[y] * here[y + 1])
+            new[y0 + y, pl.ds(HALO + i, 8, stride=STRIDE), :] = value
         return ahead, diagonal[1:]
 
     behind = [load(old, y, -1) for y in range(count)]
@@ -164,7 +171,7 @@
         pltpu.make_async_copy(weight.at[pl.ds(n * per, per)], weights.at[pl.ds(n * per, per)], weight_sem.at[n])
         for n in range(WEIGHT_CHUNKS)
     ]
-    for copy in loads + kappa_loads + [mask_load] + state_loads + surface_loads + weight_loads:
+    for copy in loads + surface_loads + weight_loads + kappa_loads + [mask_load] + state_loads:
         copy.start()
 
     barrier = pltpu.get_barrier_semaphore()
@@ -191,7 +198,7 @@
             greet(i // TILES, lax.rem(i + tile, TILES))
             return carry
 
-        lax.fori_loop(0, OCEAN * TILES, body, 0)
+        lax.fori_loop(0, OCEAN * TILES, body, 0, unroll=8)
 
     @pl.when(jnp.logical_not(is_ocean))
     def _():
@@ -199,7 +206,7 @@
             greet(OCEAN, lax.rem(i + tile, TILES))
             return carry
 
-        lax.fori_loop(0, TILES, body, 0)
+        lax.fori_loop(0, TILES, body, 0, unroll=8)
 
     received[:, PAIR:, :] = jnp.zeros((received.shape[0], 8 - PAIR, received.shape[2]), F32)
 
@@ -216,123 +223,6 @@
         planes[SEA, j, pl.ds(HALO, BY), :] = jnp.maximum(
             mask_in[:, j * BLK : (j + 1) * BLK].astype(F32), 1.0 - ocean_f
         )
-
-    sides_in = has_up.astype(jnp.int32) + has_down.astype(jnp.int32)
-    pl.semaphore_wait(barrier, jnp.where(is_ocean, OCEAN * TILES + 2, TILES + 2 + 3 * sides_in))
-
-    def remote(source, target, sems, n, device):
-        return pltpu.make_async_remote_copy(
-            src_ref=source,
-            dst_ref=target,
-            send_sem=sems.at[0, n],
-            recv_sem=sems.at[1, n],
-            device_id=device,
-            device_id_type=MESH,
-        )
-
-    def row_copies(cut, sems, n):
-        return [
-            (has_up, has_down, remote(cut(TOP - HALO), cut(0), sems, n, (comp + 1, tile))),
-            (has_down, has_up, remote(cut(HALO), cut(TOP), sems, n + 1, (comp - 1, tile))),
-        ]
-
-    def column_copies(source, target, sems, n):
-        out = []
-        for side, there in ((0, left), (1, right)):
-            out += [
-                (None, None, remote(source(side, HALO, BY), target(side, HALO, BY), sems, n, (comp, there))),
-                (has_up, has_down, remote(
-                    source(side, TOP - HALO, HALO), target(side, 0, HALO), sems, n + 1, (comp + 1, there))),
-                (has_down, has_up, remote(
-                    source(side, HALO, HALO), target(side, TOP, HALO), sems, n + 2, (comp - 1, there))),
-            ]
-            n += 3
-        return out
-
-    def each(copies, pick, act):
-        for entry in copies:
-            cond, copy = entry[pick], entry[2]
-            if cond is None:
-                act(copy)()
-            else:
-                pl.when(cond)(act(copy))
-
-    def start(copies):
-        each(copies, 0, lambda copy: copy.start)
-
-    def wait_recv(copies):
-        each(copies, 1, lambda copy: copy.wait_recv)
-
-    def wait_send(copies):
-        each(copies, 0, lambda copy: copy.wait_send)
-
-    def plane_rows(first, number):
-        return lambda y: planes.at[pl.ds(first, number), pl.ds(0, COLS), pl.ds(y, HALO), :]
-
-    def plane_edge(first, number):
-        return lambda side, y, rows: planes.at[pl.ds(first, number), side * (COLS - 1), pl.ds(y, rows), :]
-
-    def side_edge(first, number):
-        return lambda side, y, rows: sides.at[side, pl.ds(first, number), pl.ds(y, rows), :]
-
-    early = row_copies(plane_rows(KAPPA, 1), row_sem, 0) + column_copies(
-        plane_edge(KAPPA, 2), side_edge(KAPPA, 2), side_sem, 0
-    )
-    start(early)
-
-    deep_rows = []
-    for j in range(COLS):
-        for up, down, base, at, there, n in (
-            (has_up, has_down, BY - HALO, BY, comp + 1, 4 + j),
-            (has_down, has_up, 0, TOP, comp - 1, 4 + COLS + j),
-        ):
-            deep_rows.append((up, down, remote(
-                state.at[pl.ds(COUPLED, DEEP), pl.ds(base, HALO), pl.ds(j * BLK, BLK)],
-                natural.at[j, pl.ds(0, DEEP), pl.ds(at, HALO), :],
-                row_sem, n, (there, tile),
-            )))
-    start(deep_rows[:COLS])
-
-    for copy in state_loads:
-        copy.wait()
-    flat = as_rows(natural)
-
-    def turn(source, target):
-        for j in range(HALF):
-            parts = []
-            for slab in (j, j + HALF):
-                sea = planes[SEA, slab, pl.ds(target, 1), :] > 0.0
-                for g in range(LANES // 8):
-                    parts.append(jnp.where(sea, flat[level_rows(slab, g, source), :], 0.0))
-            field[target, pl.ds(FIRST + j * BLK, BLK), :] = jnp.concatenate(parts, axis=0).T
-
-    def turn_rows(source, target, number):
-        def one(i, carry):
-            turn(source + i, target + i)
-            return carry
-
-        lax.fori_loop(0, number, one, 0, unroll=4)
-
-    def turn_back(y, carry):
-        for j in range(HALF):
-            back = field[HALO + y, pl.ds(FIRST + j * BLK, BLK), :].T
-            for h, slab in enumerate((j, j + HALF)):
-                sea = planes[SEA, slab, pl.ds(HALO + y, 1), :] > 0.0
-                for g in range(LANES // 8):
-                    at = level_rows(slab, g, y)
-                    piece = back[h * LANES + g * 8 : h * LANES + g * 8 + 8]
-                    flat[at, :] = jnp.where(sea, piece, flat[at, :])
-        return carry
-
-    turn_rows(0, HALO, BY)
-    deep_sides = column_copies(
-        lambda side, y, rows: field.at[pl.ds(y, rows), pl.ds(LAST - HALO if side else FIRST, HALO), :],
-        lambda side, y, rows: ends.at[side, pl.ds(y, rows), pl.ds(HALO if side else 0, HALO), :],
-        side_sem, 6,
-    )
-    start(deep_sides)
-
-    start(deep_rows[COLS:])
 
     for copy in loads + surface_loads:
         copy.wait()
@@ -363,7 +253,7 @@
     code_high = jnp.floor(code * (1.0 / 32.0))
     code_low = code - 32.0 * code_high
     code_slot = slot_iota == jnp.where(active, tile_row * 8.0 + CAP, -1.0)
-    lane_base = (lax.rem(tile, GROUP) * 8).astype(F32)
+    lane_base = (jnp.where(is_ocean, tile // 2, lax.rem(tile, GROUP)) * 8).astype(F32)
     spots = (iota((BLK, BLK), 1).astype(F32) == lane_base + order_col).astype(BF16)
     codes = 32.0 * dot(jnp.where(code_slot, code_high, 0.0).astype(BF16), spots) + dot(
         jnp.where(code_slot, code_low, 0.0).astype(BF16), spots
@@ -387,37 +277,156 @@
     buckets = jnp.concatenate([buckets[:, :BLK] + codes, buckets[:, BLK:]], axis=1)
     send[...] = buckets.reshape(TILES, 8, COUPLED * BLK)
 
-    @pl.when(is_ocean)
-    def _():
-        def body(i, carry):
-            t = lax.rem(i + tile, TILES)
-            pltpu.make_async_remote_copy(
-                src_ref=send.at[t, pl.ds(0, PAIR)],
-                dst_ref=received.at[tile, pl.ds(0, PAIR)],
-                send_sem=remap_send,
-                recv_sem=remap_recv,
-                device_id=(i // TILES, t),
-                device_id_type=MESH,
-            ).start()
+    sides_in = has_up.astype(jnp.int32) + has_down.astype(jnp.int32)
+    pl.semaphore_wait(barrier, jnp.where(is_ocean, OCEAN * TILES + 2, TILES + 2 + 3 * sides_in))
+
+    def remote(source, target, sems, n, device):
+        return pltpu.make_async_remote_copy(
+            src_ref=source,
+            dst_ref=target,
+            send_sem=sems.at[0, n],
+            recv_sem=sems.at[1, n],
+            device_id=device,
+            device_id_type=MESH,
+        )
+
+    def row_copies(cut, sems, n):
+        return [
+            (has_up, has_down, remote(cut(TOP - HALO), cut(0), sems, n, (comp + 1, tile))),
+            (has_down, has_up, remote(cut(HALO), cut(TOP), sems, n + 1, (comp - 1, tile))),
+        ]
+
+    def column_copies(source, target, sems, n):
+        out = []
+        for side, there in ((0, left), (1, right)):
+            out += [
+                (None, None, remote(source(side, HALO, BY), target(side, HALO, BY), sems, n, (comp, there))),
+                (has_up, has_down, remote(
+                    source(side, TOP - HALO, HALO), target(side, 0, HALO), sems, n + 1, (comp + 1, there))),
+                (has_down, has_up, remote(
+                    source(side, HALO, HALO), target(side, TOP, HALO), sems, n + 2, (comp - 1, there))),
+            ]
+            n += 3
+        return out
+
+    def each(copies, pick, act):
+        for entry in copies:
+            cond, copy = entry[pick], entry[2]
+            if cond is None:
+                act(copy)()
+            else:
+                pl.when(cond)(act(copy))
+
+    def start(copies):
+        each(copies, 0, lambda copy: copy.start)
+
+    def wait_recv(copies):
+        each(copies, 1, lambda copy: copy.wait_recv)
+
+    def wait_send(copies):
+        each(copies, 0, lambda copy: copy.wait_send)
+
+    def plane_rows(first, number):
+        return lambda y: planes.at[pl.ds(first, number), pl.ds(0, COLS), pl.ds(y, HALO), :]
+
+    def plane_edge(first, number):
+        return lambda side, y, rows: planes.at[pl.ds(first, number), side * (COLS - 1), pl.ds(y, rows), :]
+
+    def side_edge(first, number):
+        return lambda side, y, rows: sides.at[side, pl.ds(first, number), pl.ds(y, rows), :]
+
+    early = row_copies(plane_rows(KAPPA, 1), row_sem, 0) + column_copies(
+        plane_edge(KAPPA, 2), side_edge(KAPPA, 2), side_sem, 0
+    )
+    start(early)
+
+    def send_remap(first, last):
+        @pl.when(is_ocean)
+        def _():
+            def body(i, carry):
+                t = lax.rem((i // 2) * 5 + tile + 16, TILES)
+                pltpu.make_async_remote_copy(
+                    src_ref=send.at[t, pl.ds(0, PAIR)],
+                    dst_ref=received.at[lax.rem(tile, 2) * PASSED + tile // 2, pl.ds(0, PAIR)],
+                    send_sem=remap_send,
+                    recv_sem=remap_recv,
+                    device_id=(jnp.where(lax.rem(i, 2) == 0, lax.rem(tile, 2), OCEAN - 1), t),
+                    device_id_type=MESH,
+                ).start()
+                return carry
+
+            lax.fori_loop(2 * first, 2 * last, body, 0, unroll=8)
+
+        @pl.when(jnp.logical_not(is_ocean))
+        def _():
+            def body(i, carry):
+                t = lax.rem(i * 5 + tile + 16, TILES)
+                pltpu.make_async_remote_copy(
+                    src_ref=send.at[t, pl.ds(0, PAIR)],
+                    dst_ref=received.at[comp * TILES + tile, pl.ds(0, PAIR)],
+                    send_sem=remap_send,
+                    recv_sem=remap_recv,
+                    device_id=(OCEAN, t),
+                    device_id_type=MESH,
+                ).start()
+                return carry
+
+            lax.fori_loop(first, last, body, 0, unroll=8)
+
+    deep_rows = []
+    for j in range(COLS):
+        for up, down, base, at, there, n in (
+            (has_up, has_down, BY - HALO, BY, comp + 1, 4 + j),
+            (has_down, has_up, 0, TOP, comp - 1, 4 + COLS + j),
+        ):
+            deep_rows.append((up, down, remote(
+                state.at[pl.ds(COUPLED, DEEP), pl.ds(base, HALO), pl.ds(j * BLK, BLK)],
+                natural.at[j, pl.ds(0, DEEP), pl.ds(at, HALO), :],
+                row_sem, n, (there, tile),
+            )))
+    send_remap(0, PART)
+    start(deep_rows[: 2 * SLABS])
+
+    for copy in state_loads:
+        copy.wait()
+    flat = as_rows(natural)
+
+    def turn(source, target):
+        for j in range(HALF):
+            parts = []
+            for slab in (j, j + HALF):
+                sea = planes[SEA, slab, pl.ds(target, 1), :] > 0.0
+                for g in range(LANES // 8):
+                    parts.append(jnp.where(sea, flat[level_rows(slab, g, source), :], 0.0))
+            field[target, pl.ds(FIRST + j * BLK, BLK), :] = jnp.concatenate(parts, axis=0).T
+
+    def turn_rows(source, target, number):
+        def one(i, carry):
+            turn(source + i, target + i)
             return carry
 
-        lax.fori_loop(0, OCEAN * TILES, body, 0)
-
-    @pl.when(jnp.logical_not(is_ocean))
-    def _():
-        def body(i, carry):
-            t = lax.rem(i + tile, TILES)
-            pltpu.make_async_remote_copy(
-                src_ref=send.at[t, pl.ds(0, PAIR)],
-                dst_ref=received.at[comp * TILES + tile, pl.ds(0, PAIR)],
-                send_sem=remap_send,
-                recv_sem=remap_recv,
-                device_id=(OCEAN, t),
-                device_id_type=MESH,
-            ).start()
-            return carry
-
-        lax.fori_loop(0, TILES, body, 0)
+        lax.fori_loop(0, number, one, 0, unroll=4)
+
+    def turn_back(y, carry):
+        for j in range(HALF):
+            back = field[HALO + y, pl.ds(FIRST + j * BLK, BLK), :].T
+            for h, slab in enumerate((j, j + HALF)):
+                sea = planes[SEA, slab, pl.ds(HALO + y, 1), :] > 0.0
+                for g in range(LANES // 8):
+                    at = level_rows(slab, g, y)
+                    piece = back[h * LANES + g * 8 : h * LANES + g * 8 + 8]
+                    flat[at, :] = jnp.where(sea, piece, flat[at, :])
+        return carry
+
+    turn_rows(0, HALO, BY)
+    deep_sides = column_copies(
+        lambda side, y, rows: field.at[pl.ds(y, rows), pl.ds(LAST - HALO if side else FIRST, HALO), :],
+        lambda side, y, rows: ends.at[side, pl.ds(y, rows), pl.ds(HALO if side else 0, HALO), :],
+        side_sem, 6,
+    )
+    start(deep_sides)
+
+    send_remap(PART, TILES)
 
     wait_recv(early)
     lane = iota((TALL, BLK), 1)
@@ -429,31 +438,42 @@
     sea = wide(planes, SEA)
     scale = jnp.where(sea > 0.0, wide(planes, KAPPA), 0.0)
     middle = 1.0 - scale * neighbours(sea)
+    ends_of = []
     for n, value in enumerate((middle, scale)):
         tiles = [value[:, j * BLK : (j + 1) * BLK] for j in range(COLS + 1)]
         for j in range(COLS + 1):
             coef[n, j] = tiles[j]
-        coef[n, COLS + 1] = jnp.where(lane < BLK // 2, tiles[HALF], tiles[COLS])
-        coef[n, COLS + 2] = jnp.where(lane < BLK // 2, tiles[COLS], tiles[HALF - 1])
-
-    def spread_row(y, carry):
-        for n, target in enumerate((centre, around)):
-            for a, b, at in [(j, j + HALF, FIRST + j * BLK) for j in range(HALF)] + [(COLS + 1, COLS + 2, None)]:
-                both = jnp.concatenate(
-                    [
-                        jnp.broadcast_to(coef[n, a, pl.ds(y, 1), :], (LANES, BLK)),
-                        jnp.broadcast_to(coef[n, b, pl.ds(y, 1), :], (LANES, BLK)),
-                    ],
-                    axis=0,
-                ).T
-                if at is None:
-                    target[y, pl.ds(LAST, 8), :] = both[:8]
-                    target[y, pl.ds(0, 8), :] = both[BLK - 8 :]
-                else:
-                    target[y, pl.ds(at, BLK), :] = both
-        return carry
-
-    lax.fori_loop(0, TALL, spread_row, 0, unroll=2)
+        ends_of.append([
+            jnp.where(lane < BLK // 2, tiles[HALF], tiles[COLS]),
+            jnp.where(lane < BLK // 2, tiles[COLS], tiles[HALF - 1]),
+        ])
+    for h in range(2):
+        inner = jnp.where(lane < BLK // 2, pltpu.roll(ends_of[1][h], 8, 1), pltpu.roll(ends_of[1][h], BLK - 8, 1))
+        coef[h, COLS + 1] = jnp.where((lane < HALO) | (lane >= BLK - HALO), ends_of[0][h], inner)
+
+    def spread(first, second, y):
+        halves = [jnp.broadcast_to(coef[n, j, pl.ds(y, 1), :], (LANES, BLK)) for n, j in (first, second)]
+        return jnp.concatenate(halves, axis=0).T
+
+    def spread_rows(first, last, targets):
+        def one(y, carry):
+            for n, target in targets:
+                for j in range(HALF):
+                    target[y, pl.ds(FIRST + j * BLK, BLK), :] = spread((n, j), (n, j + HALF), y)
+            both = spread((0, COLS + 1), (1, COLS + 1), y)
+            for n, target in targets:
+                target[y, pl.ds(LAST, 8), :] = both[8 * n : 8 * n + 8]
+                target[y, pl.ds(0, 8), :] = both[BLK - 8 - 8 * n : BLK - 8 * n]
+            return carry
+
+        lax.fori_loop(first, last, one, 0, unroll=2)
+
+    in_ocean = pl.when(is_ocean)
+    in_air = pl.when(jnp.logical_not(is_ocean))
+    in_ocean(lambda: spread_rows(HALO, TOP, ((0, centre), (1, around))))
+    in_air(lambda: spread_rows(1, TALL - 1, ((1, around),)))
+
+    start(deep_rows[2 * SLABS :])
 
     def join(y, carry):
         low = iota((8, BLK), 1) < LANES
@@ -465,16 +485,51 @@
 
     wait_recv(deep_sides)
     lax.fori_loop(HALO, TOP, join, 0, unroll=4)
-    step_blocks(field, other, around, centre, 5, 10, 25, 3)
+    def four(y):
+        return 4.0
+
+    def faces(y):
+        shut = ((comp == 0) & (y == HALO)) | ((comp == OCEAN - 1) & (y == TOP - 1))
+        return jnp.where(shut, 3.0, 4.0)
+
+    def sea_step(old, new):
+        step_blocks(old, new, around, centre, HALO, 8, TOP - 8, 4)
+
+    @in_ocean
+    def _():
+        for y in (HALO - 1, TOP):
+            field[y] = jnp.zeros((LONG, BLK), F32)
+            other[y] = jnp.zeros((LONG, BLK), F32)
+        sea_step(field, other)
+
+    @in_air
+    def _():
+        step_blocks(field, other, around, four, 5, 10, 25, 3)
+
     wait_send(deep_sides)
-    step_blocks(other, field, around, centre, 6, 7, 27, 4)
-    step_blocks(field, other, around, centre, 7, 9, 24, 3)
-    step_blocks(other, field, around, centre, 8, 8, 24, 3)
-    lax.fori_loop(HALO, BY - HALO, turn_back, 0, unroll=4)
+
+    @in_ocean
+    def _():
+        sea_step(other, field)
+        sea_step(field, other)
+
+    @in_air
+    def _():
+        step_blocks(other, field, around, four, 6, 7, 27, 4)
+
+    mine = received.at[pl.ds(jnp.minimum(comp, 1) * PASSED, PASSED), pl.ds(0, PAIR)]
+    passed = remote(mine, mine, side_sem, 18, (jnp.where(comp == 0, 1, 0), tile))
+
+    @pl.when(comp < OCEAN - 1)
+    def _():
+        pltpu.make_async_copy(mine, mine, remap_recv).wait()
+        passed.start()
+
+    @in_air
+    def _():
+        step_blocks(field, other, around, four, 7, 9, 24, 3)
 
     def accumulate(sources):
-        whole = received.at[pl.ds(0, sources), pl.ds(0, PAIR)]
-        pltpu.make_async_copy(whole, whole, remap_recv).wait()
         heads = received[pl.ds(0, sources), CAP, :BLK]
         offset = 1.0 + BLOCKS * comp.astype(F32)
         total = jnp.zeros((BLOCKS, COUPLED * BLK), F32)
@@ -492,6 +547,13 @@
                 new = total[j * BY : (j + 1) * BY, f * BLK : (f + 1) * BLK]
                 planes[f, j, pl.ds(HALO, BY), :] = old + weight_here * (new - old)
 
+    def arrived(sources):
+        whole = received.at[pl.ds(0, sources), pl.ds(0, PAIR)]
+        pltpu.make_async_copy(whole, whole, remap_recv).wait()
+
+    pl.when(comp == OCEAN - 1)(lambda: arrived(TILES))
+    pl.when(comp < OCEAN - 1)(passed.wait_recv)
+    in_ocean(lambda: arrived(OCEAN * TILES))
     pl.when(is_ocean)(lambda: accumulate(OCEAN * TILES))
     pl.when(jnp.logical_not(is_ocean))(lambda: accumulate(TILES))
 
@@ -499,6 +561,15 @@
         plane_edge(0, COUPLED), side_edge(0, COUPLED), side_sem, 12
     )
     start(late)
+    @in_ocean
+    def _():
+        sea_step(other, field)
+
+    @in_air
+    def _():
+        step_blocks(other, field, around, four, 8, 8, 24, 3)
+
+    lax.fori_loop(HALO, BY - HALO, turn_back, 0, unroll=4)
 
     wait_recv(deep_rows)
 
@@ -512,18 +583,20 @@
         turn_rows(TOP, TOP, HALO)
         lax.fori_loop(TOP, TALL, join, 0, unroll=4)
 
-    @pl.when(jnp.logical_not(has_down))
+    @pl.when(comp == 0)
     def _():
         field[pl.ds(0, HALO)] = jnp.zeros((HALO, LONG, BLK), F32)
 
-    @pl.when(jnp.logical_not(has_up))
+    @pl.when(comp == OCEAN - 1)
     def _():
         field[pl.ds(TOP, HALO)] = jnp.zeros((HALO, LONG, BLK), F32)
 
-    step_outer(field, other, around, centre, 1)
-    step_outer(other, field, around, centre, 2)
-    step_outer(field, other, around, centre, 3)
-    step_outer(other, field, around, centre, 4)
+    @in_air
+    def _():
+        step_outer(field, other, around, faces, 1)
+        step_outer(other, field, around, faces, 2)
+        step_outer(field, other, around, faces, 3)
+        step_outer(other, field, around, faces, 4)
 
     def turn_back_outer(i, carry):
         return turn_back(jnp.where(i < HALO, i, i + BY - 2 * HALO), carry)
@@ -534,10 +607,11 @@
     wait_send(early)
     wait_send(late)
     wait_send(deep_rows)
+    pl.when(comp < OCEAN - 1)(passed.wait_send)
 
     @pl.when(is_ocean)
     def _():
-        whole = received.at[:, pl.ds(0, PAIR)]
+        whole = received.at[pl.ds(0, 2 * TILES), pl.ds(0, PAIR)]
         pltpu.make_async_copy(whole, whole, remap_send).wait()
 
     @pl.when(jnp.logical_not(is_ocean))
@@ -580,7 +654,7 @@
         pltpu.VMEM((COLS, LANES, TALL, BLK), F32),
         pltpu.VMEM((5, COLS + 1, TALL, BLK), F32),
         pltpu.VMEM((2, 5, TALL, BLK), F32),
-        pltpu.VMEM((2, COLS + 3, TALL, BLK), F32),
+        pltpu.VMEM((2, COLS + 2, TALL, BLK), F32),
     )
     operands = (
         state, kappa, land_mask, remap_weight,
@@ -611,7 +685,7 @@
             dma,
             dma,
             dma((2, 4 + 2 * COLS)),
-            dma((2, 18)),
+            dma((2, 19)),
         ],
         compiler_params=pltpu.CompilerParams(
             collective_id=0, has_side_effects=True, vmem_limit_bytes=44 << 20

time: 41.2 us -> 38.2 us (0.927)
  Pallas kernels: 40.5 us -> 37.5 us
    pallas_call x1, Pallas kernels: 37.9 us -> 34.9 us  [shards(): pl.pallas_call(exchange_kernel, out_shape=kept, in_specs=[hbm] * 7 + [pl....]
where the time goes in v2:
time: 38.2 us; the launch traced here: 38.1 us
  Pallas kernels  37.5 us (98%)
  between operations  0.66 us (2%)
    pallas_call x1, Pallas kernels, shards(): pl.pallas_call(exchange_kernel, out_shape=kept, in_specs=[hbm] * 7 + [pl....  34.9 us
    pallas_call x1, Pallas kernels, shards(): pl.pallas_call(finish_kernel, out_shape=jax.ShapeDtypeStruct((LEVELS, BY,...  2.6 us

profile of v2, /device:TPU:1, one launch (start us, length us, event | category | flops | bytes accessed | tf_op | source)
XLA Modules:
  0.0 38.1 jit_solution(14388559020011585482)
XLA Ops:
  0.7 34.9 %exchange.1 = (f32[6,64,40,128]{3,2,1,0:T(8,128)S(1)}, f32[5,7,40,128]{3,2,1,0:T(8,128)S(1)}, f32[2,5,40,128]{3,2,1,0:T(8,128)S(1)}, f32[2,8,40,128]{3,2,1,0:T(8,128)S(1)}) custom-call(f32[60,32,768]{2,1,0:T(8,128)} %state.1, f32[32,768]{1,0:T(8,128)} %kappa.1, s32[32,768]{1,0:T(8,128)} %mask.1, bf16[128,128,128]{2,1,0:T(8,128)(2,1)} %weight.1, ...), custom_call_target="tpu_custom_call" | custom-call | tf_op jit(solution)/shard_map/exchange/pallas_call | solution.py:665
  35.5 2.6 %finish.1 = f32[60,32,768]{2,1,0:T(8,128)} custom-call(f32[6,64,40,128]{3,2,1,0:T(8,128)S(1)} %get-tuple-element.9.natural, f32[5,7,40,128]{3,2,1,0:T(8,128)S(1)} %get-tuple-element.10.planes, f32[2,5,40,128]{3,2,1,0:T(8,128)S(1)} %get-tuple-element.11.sides, f32[2,8,40,128]{3,2,1,0:T(8,128)S(1)} %get-tuple-element.12.coef), custom_call_target="tpu_custom_call" | custom-call | tf_op jit(solution)/shard_map/finish/pallas_call | solution.py:695

commit v3 on v2

--- a/solution.py
+++ b/solution.py
@@ -427,6 +427,7 @@
     start(deep_sides)
 
     send_remap(PART, TILES)
+    start(deep_rows[2 * SLABS :])
 
     wait_recv(early)
     lane = iota((TALL, BLK), 1)
@@ -472,8 +473,6 @@
     in_air = pl.when(jnp.logical_not(is_ocean))
     in_ocean(lambda: spread_rows(HALO, TOP, ((0, centre), (1, around))))
     in_air(lambda: spread_rows(1, TALL - 1, ((1, around),)))
-
-    start(deep_rows[2 * SLABS :])
 
     def join(y, carry):
         low = iota((8, BLK), 1) < LANES

time: 38.2 us -> 37.4 us (0.979)
  the two profiles are of different devices: /device:TPU:1 before, /device:TPU:5 now
where the time goes in v3:
time: 37.4 us; the launch traced here: 37.3 us
  Pallas kernels  36.7 us (98%)
  between operations  0.66 us (2%)
    pallas_call x1, Pallas kernels, shards(): pl.pallas_call(exchange_kernel, out_shape=kept, in_specs=[hbm] * 7 + [pl....  34.1 us
    pallas_call x1, Pallas kernels, shards(): pl.pallas_call(finish_kernel, out_shape=jax.ShapeDtypeStruct((LEVELS, BY,...  2.6 us

profile of v3, /device:TPU:5, one launch (start us, length us, event | category | flops | bytes accessed | tf_op | source)
XLA Modules:
  0.0 37.3 jit_solution(5440006348430593049)
XLA Ops:
  0.7 34.1 %exchange.1 = (f32[6,64,40,128]{3,2,1,0:T(8,128)S(1)}, f32[5,7,40,128]{3,2,1,0:T(8,128)S(1)}, f32[2,5,40,128]{3,2,1,0:T(8,128)S(1)}, f32[2,8,40,128]{3,2,1,0:T(8,128)S(1)}) custom-call(f32[60,32,768]{2,1,0:T(8,128)} %state.1, f32[32,768]{1,0:T(8,128)} %kappa.1, s32[32,768]{1,0:T(8,128)} %mask.1, bf16[128,128,128]{2,1,0:T(8,128)(2,1)} %weight.1, ...), custom_call_target="tpu_custom_call" | custom-call | tf_op jit(solution)/shard_map/exchange/pallas_call | solution.py:664
  34.7 2.6 %finish.1 = f32[60,32,768]{2,1,0:T(8,128)} custom-call(f32[6,64,40,128]{3,2,1,0:T(8,128)S(1)} %get-tuple-element.9.natural, f32[5,7,40,128]{3,2,1,0:T(8,128)S(1)} %get-tuple-element.10.planes, f32[2,5,40,128]{3,2,1,0:T(8,128)S(1)} %get-tuple-element.11.sides, f32[2,8,40,128]{3,2,1,0:T(8,128)S(1)} %get-tuple-element.12.coef), custom_call_target="tpu_custom_call" | custom-call | tf_op jit(solution)/shard_map/finish/pallas_call | solution.py:694
